TPU v7x, 512 devices: a whole 4x8x8 slice. The times are simulated.
512 devices in a mesh: kx: 4 (over z_lo), ky: 4 (over x), kz: 4 (over z_hi, core), fft: 8 (over y).
Axes of the slice: x: 4, y: 8, z: 8 (z_hi: 2, z_lo: 4; z = z_hi * 4 + z_lo), core: 2. Of those that a mesh axis runs over, the one named last changes fastest.
Arguments:
- occupied: bfloat16 [4, 4, 4, 2, 2, 96, 96, 128], P('kx', 'ky', 'kz', None, None, 'fft'), may hold values from -6 to 6
- targets: bfloat16 [4, 4, 4, 2, 2, 96, 96, 128], P('kx', 'ky', 'kz', None, None, 'fft'), may hold values from -6 to 6
- weights: bfloat16 [4, 4, 4, 2], P('kx', 'ky', 'kz'), may hold values from 0.19921875 to 2
- kernel: bfloat16 [96, 96, 128], P(None, 'fft'), may hold values from 0.099609375 to 4
Outputs:
- exchanged: bfloat16 [4, 4, 4, 2, 2, 96, 96, 128], P('kx', 'ky', 'kz', None, None, 'fft')
All inputs are finite; a program needn't handle non-finite values.
Results may differ from a plain program's by a relative error of at most 0.0095.
Values may be sent and summed in bfloat16 or wider, within the bound.
A program may use at most 64 MiB of HBM per device.

v0:
```python
import math

import jax
import jax.numpy as jnp
from jax import lax
from jax.sharding import PartitionSpec as P


def shifted(value, axis, by):
    size = lax.axis_size(axis)
    return lax.ppermute(value, axis, [(i, (i + by) % size) for i in range(size)])


def dft_table(length, sign):
    index = jnp.arange(length, dtype=jnp.int32)
    phase = index[:, None] * index[None, :] % length
    theta = phase.astype(jnp.float32) * (2.0 * math.pi / length)
    factor = 1.0 / math.sqrt(length)
    cosine = jnp.cos(theta) * factor
    sine = jnp.sin(theta) * (sign * factor)
    return jnp.stack([jnp.stack([cosine, -sine]), jnp.stack([sine, cosine])]).astype(jnp.bfloat16)


def transform(field, table, form):
    return jnp.einsum(form, table, field, preferred_element_type=jnp.float32)


def shards(occupied, targets, weights, kernel):
    occ = occupied[0, 0, 0]
    tgt = targets[0, 0, 0]
    wts = weights[0, 0, 0]
    occ, wts = shifted((occ, wts), "kx", 1)
    occ, wts = shifted((occ, wts), "ky", 1)
    occ, wts = shifted((occ, wts), "kz", 1)
    occ_count = occ.shape[1]
    tgt_count = tgt.shape[1]
    planes = occ.shape[2]
    width_a = kernel.shape[0]
    width_b = occ.shape[3]
    width_c = occ.shape[4]
    occ_re = occ[0][:, None].astype(jnp.float32)
    occ_im = occ[1][:, None].astype(jnp.float32)
    tgt_re = tgt[0][None].astype(jnp.float32)
    tgt_im = tgt[1][None].astype(jnp.float32)
    pair = jnp.stack([occ_re * tgt_re + occ_im * tgt_im, occ_re * tgt_im - occ_im * tgt_re]).astype(
        jnp.bfloat16
    )
    pair = pair.reshape((2, occ_count * tgt_count, planes, width_b, width_c))
    first = transform(pair, dft_table(width_c, -1.0), "oikj,ipabj->opabk").astype(jnp.bfloat16)
    second = transform(first, dft_table(width_b, -1.0), "oikj,ipajc->opakc").astype(jnp.bfloat16)
    forward_a = dft_table(width_a, -1.0)
    inverse_a = dft_table(width_a, 1.0)
    spectrum = transform(
        lax.all_to_all(second, "fft", split_axis=3, concat_axis=2, tiled=True),
        forward_a,
        "oikj,ipjbc->opkbc",
    )
    screened = (spectrum * kernel).astype(jnp.bfloat16)
    back_one = transform(screened, inverse_a, "oikj,ipjbc->opkbc").astype(jnp.bfloat16)
    returned = lax.all_to_all(back_one, "fft", split_axis=2, concat_axis=3, tiled=True)
    back_two = transform(returned, dft_table(width_b, 1.0), "oikj,ipajc->opakc").astype(
        jnp.bfloat16
    )
    potential = transform(back_two, dft_table(width_c, 1.0), "oikj,ipabj->opabk")
    potential = potential.reshape((2, occ_count, tgt_count, planes, width_b, width_c))
    scaled = wts.astype(jnp.float32)[:, None, None, None, None]
    orb_re = occ[0].astype(jnp.float32)[:, None] * scaled
    orb_im = occ[1].astype(jnp.float32)[:, None] * scaled
    real_part = jnp.sum(orb_re * potential[0] - orb_im * potential[1], axis=0)
    imag_part = jnp.sum(orb_re * potential[1] + orb_im * potential[0], axis=0)
    result = (-0.25 * jnp.stack([real_part, imag_part])).astype(jnp.bfloat16)
    return result[None, None, None]


def solution(mesh):
    return jax.shard_map(
        shards,
        mesh=mesh,
        in_specs=(
            P("kx", "ky", "kz", None, None, "fft", None, None),
            P("kx", "ky", "kz", None, None, "fft", None, None),
            P("kx", "ky", "kz", None),
            P(None, "fft", None),
        ),
        out_specs=P("kx", "ky", "kz", None, None, "fft", None, None),
        check_vma=False,
    )
```

profile of v0, /device:TPU:1, one launch (start us, length us, event | category | flops | bytes accessed | tf_op | source)
XLA Modules:
  0.0 250.9 jit_solution(8061267059879132527)
XLA Ops:
  0.0 4.8 %collective-permute-start = (bf16[2,2,12,96,128]{4,3,2,1,0:T(8,128)(2,1)}, bf16[2,2,12,96,128]{4,3,2,1,0:T(8,128)(2,1)S(1)}, u32[]{:S(2)}, u32[]{:S(2)}) collective-permute-start(bf16[2,2,12,96,128]{4,3,2,1,0:T(8,128)(2,1)} %bitcast.174), channel_id=1, source_target_pairs={{0,128},{128,256},{256,384},{384,0},{1,129},{129,257},{257,385},{3... | collective-permute-start | bytes 3538952 | tf_op jit(solution)/shard_map/ppermute | solution.py:11
  4.8 26.2 %collective-permute-done = bf16[2,2,12,96,128]{4,3,2,1,0:T(8,128)(2,1)S(1)} collective-permute-done((bf16[2,2,12,96,128]{4,3,2,1,0:T(8,128)(2,1)}, bf16[2,2,12,96,128]{4,3,2,1,0:T(8,128)(2,1)S(1)}, u32[]{:S(2)}, u32[]{:S(2)}) %collective-permute-start) | collective-permute-done | bytes 1179680 | tf_op jit(solution)/shard_map/ppermute | solution.py:11
  31.0 6.4 %collective-permute-start.1 = (bf16[2,2,12,96,128]{4,3,2,1,0:T(8,128)(2,1)S(1)}, bf16[2,2,12,96,128]{4,3,2,1,0:T(8,128)(2,1)S(1)}, u32[]{:S(2)}, u32[]{:S(2)}) collective-permute-start(bf16[2,2,12,96,128]{4,3,2,1,0:T(8,128)(2,1)S(1)} %collective-permute-done), channel_id=1, source_target_pairs={{0,32},{32,64},{64,96},{96,0},{1,33},{33,65},{65,97},{97,1},{2,34}... | collective-permute-start | bytes 3538952 | tf_op jit(solution)/shard_map/ppermute | solution.py:11
  37.4 25.8 %collective-permute-done.1 = bf16[2,2,12,96,128]{4,3,2,1,0:T(8,128)(2,1)S(1)} collective-permute-done((bf16[2,2,12,96,128]{4,3,2,1,0:T(8,128)(2,1)S(1)}, bf16[2,2,12,96,128]{4,3,2,1,0:T(8,128)(2,1)S(1)}, u32[]{:S(2)}, u32[]{:S(2)}) %collective-permute-start.1) | collective-permute-done | bytes 1179680 | tf_op jit(solution)/shard_map/ppermute | solution.py:11
  63.3 10.3 %collective-permute-start.2 = (bf16[2,2,12,96,128]{4,3,2,1,0:T(8,128)(2,1)S(1)}, bf16[2,2,12,96,128]{4,3,2,1,0:T(8,128)(2,1)S(1)}, u32[]{:S(2)}, u32[]{:S(2)}) collective-permute-start(bf16[2,2,12,96,128]{4,3,2,1,0:T(8,128)(2,1)S(1)} %collective-permute-done.1), channel_id=1, source_target_pairs={{0,8},{8,16},{16,24},{24,0},{1,9},{9,17},{17,25},{25,1},{2,10},{10... | collective-permute-start | bytes 3538952 | tf_op jit(solution)/shard_map/ppermute | solution.py:11
  76.5 1.5 bitcast_convert_fusion.5
  78.0 18.7 %collective-permute-done.2 = bf16[2,2,12,96,128]{4,3,2,1,0:T(8,128)(2,1)S(1)} collective-permute-done((bf16[2,2,12,96,128]{4,3,2,1,0:T(8,128)(2,1)S(1)}, bf16[2,2,12,96,128]{4,3,2,1,0:T(8,128)(2,1)S(1)}, u32[]{:S(2)}, u32[]{:S(2)}) %collective-permute-start.2) | collective-permute-done | bytes 1179680 | tf_op jit(solution)/shard_map/ppermute | solution.py:11
  98.1 1.7 add_convert_fusion
  99.8 2.9 %fusion.4 = bf16[2,4,12,96,128]{4,3,0,2,1:T(8,128)(2,1)S(1)} fusion(bf16[1,4,12,96,128]{4,3,0,2,1:T(8,128)(2,1)} %bitcast.173, bf16[1,4,12,96,128]{4,3,0,2,1:T(8,128)(2,1)S(1)} %bitcast.172, bf16[1,2,128,128]{3,2,1,0:T(8,128)(2,1)} %get-tuple-element.19, bf16[1,2,128,128]{3,2,1,0:T(8,128)(2,1)} %get-tuple-element.20, ...), kind=kOutput, calls=%fused_computation.8 | convolution fusion | flops 1064452096 | bytes 4923392 | tf_op jit(solution)/shard_map/oikj,ipajc->opakc/dot_general | solution.py:25
  102.6 3.3 %copy.9 = bf16[2,4,12,96,128]{4,0,2,1,3:T(2,128)(2,1)} copy(bf16[2,4,12,96,128]{4,3,0,2,1:T(8,128)(2,1)S(1)} %fusion.4) | data formatting | bytes 4718592 | tf_op jit(solution)/shard_map/convert_element_type | solution.py:50
  105.9 6.8 %all-to-all-start = ((bf16[2,4,12,96,128]{4,0,2,1,3:T(2,128)(2,1)}), bf16[2,4,12,96,128]{4,0,2,1,3:T(2,128)(2,1)S(1)}, u32[]{:S(2)}, u32[]{:S(2)}) async-start(bf16[2,4,12,96,128]{4,0,2,1,3:T(2,128)(2,1)} %copy.9), calls=%async_computation | async-start | bytes 4718592 | tf_op jit(solution)/shard_map/all_to_all | solution.py:54
  112.7 54.7 %all-to-all-done = bf16[2,4,12,96,128]{4,0,2,1,3:T(2,128)(2,1)S(1)} async-done(((bf16[2,4,12,96,128]{4,0,2,1,3:T(2,128)(2,1)}), bf16[2,4,12,96,128]{4,0,2,1,3:T(2,128)(2,1)S(1)}, u32[]{:S(2)}, u32[]{:S(2)}) %all-to-all-start) | async-done | bytes 2359328 | tf_op jit(solution)/shard_map/all_to_all | solution.py:54
  169.9 3.3 %fusion.5 = bf16[2,4,96,12,128]{4,2,0,3,1:T(8,128)(2,1)} fusion(f32[96,12,128]{2,0,1:T(8,128)S(1)} %convert_element_type.202, bf16[2,4,96,12,128,1]{4,1,3,2,0,5:T(4,128)(2,1)S(1)} %bitcast.171, bf16[1,2,96,96]{3,2,1,0:T(8,128)(2,1)S(1)} %copy-done.4, bf16[1,2,96,96]{3,2,1,0:T(8,128)(2,1)S(1)} %copy-done.3, bf16[1,2,96,96]{3,2,1,0:T(8,128)(2,1)S(1)} %copy-done.5, ...), kind=kOutput, calls=%fused_computation.9 | convolution fusion | flops 909803520 | bytes 5455872 | tf_op jit(solution)/shard_map/oikj,ipjbc->opkbc/dot_general | solution.py:25
  173.2 4.9 %copy.13 = bf16[2,4,96,12,128]{4,0,3,1,2:T(2,128)(2,1)} copy(bf16[2,4,96,12,128]{4,2,0,3,1:T(8,128)(2,1)} %fusion.5) | data formatting | bytes 4718592 | tf_op jit(solution)/shard_map/convert_element_type | solution.py:59
  178.1 3.7 %all-to-all-start.1 = ((bf16[2,4,96,12,128]{4,0,3,1,2:T(2,128)(2,1)}), bf16[2,4,96,12,128]{4,0,3,1,2:T(2,128)(2,1)S(1)}, u32[]{:S(2)}, u32[]{:S(2)}) async-start(bf16[2,4,96,12,128]{4,0,3,1,2:T(2,128)(2,1)} %copy.13), calls=%async_computation.1 | async-start | bytes 4718592 | tf_op jit(solution)/shard_map/all_to_all | solution.py:60
  181.9 6.3 %collective-permute-start.3 = (bf16[2]{0:T(256)(128)(2,1)S(1)}, bf16[2]{0:T(256)(128)(2,1)S(1)}, u32[]{:S(2)}, u32[]{:S(2)}) collective-permute-start(bf16[2]{0:T(256)(128)(2,1)S(1)} %bitcast.175), channel_id=1, source_target_pairs={{0,128},{128,256},{256,384},{384,0},{1,129},{129,257},{257,385},{3... | collective-permute-start | bytes 20 | tf_op jit(solution)/shard_map/ppermute | solution.py:11
  188.9 1.9 collective-permute-start.4
  190.8 3.9 %collective-permute-done.4 = bf16[2]{0:T(256)(128)(2,1)S(1)} collective-permute-done((bf16[2]{0:T(256)(128)(2,1)S(1)}, bf16[2]{0:T(256)(128)(2,1)S(1)}, u32[]{:S(2)}, u32[]{:S(2)}) %collective-permute-start.4) | collective-permute-done | bytes 36 | tf_op jit(solution)/shard_map/ppermute | solution.py:11
  194.7 1.9 collective-permute-start.5
  196.6 2.7 %collective-permute-done.5 = bf16[2]{0:T(256)(128)(2,1)S(1)} collective-permute-done((bf16[2]{0:T(256)(128)(2,1)S(1)}, bf16[2]{0:T(256)(128)(2,1)S(1)}, u32[]{:S(2)}, u32[]{:S(2)}) %collective-permute-start.5) | collective-permute-done | bytes 36 | tf_op jit(solution)/shard_map/ppermute | solution.py:11
  199.3 2.6 %broadcast_multiply_fusion.1 = (f32[2,12,96,128]{3,2,1,0:T(8,128)S(1)}, f32[2,12,96,128]{3,2,1,0:T(8,128)}) fusion(f32[2]{0:T(128)S(1)} %convert_element_type.189, bf16[2,2,12,96,128]{4,3,2,1,0:T(8,128)(2,1)} %copy-done.1), kind=kLoop, calls=%fused_computation.37 | loop fusion | flops 1179648 | bytes 3538952 | tf_op jit(solution)/shard_map/mul | solution.py:67
  201.9 37.2 %all-to-all-done.1 = bf16[2,4,96,12,128]{4,0,3,1,2:T(2,128)(2,1)S(1)} async-done(((bf16[2,4,96,12,128]{4,0,3,1,2:T(2,128)(2,1)}), bf16[2,4,96,12,128]{4,0,3,1,2:T(2,128)(2,1)S(1)}, u32[]{:S(2)}, u32[]{:S(2)}) %all-to-all-start.1) | async-done | bytes 2359328 | tf_op jit(solution)/shard_map/all_to_all | solution.py:60
  241.2 4.6 %fusion.29 = f32[2,4,12,96,128]{4,3,0,2,1:T(8,128)} fusion(bf16[2,4,12,96,128,1]{4,1,3,2,0,5:T(4,128)(2,1)S(1)} %bitcast.164, bf16[1,2,128,128]{3,2,1,0:T(8,128)(2,1)} %get-tuple-element.18, bf16[1,2,128,128]{3,2,1,0:T(8,128)(2,1)} %get-tuple-element.17, bf16[1,2,96,96]{3,2,1,0:T(8,128)(2,1)} %get-tuple-element.22, bf16[1,2,96,96]{3,2,1,0:T(8,128)(2,1)} %get-tuple-element.21), kind=kOutput, calls=%fused_computation.29 | convolution fusion | flops 1058553856 | bytes 7282688 | tf_op jit(solution)/shard_map/oikj,ipabj->opabk/dot_general | solution.py:25
  245.8 2.8 %fusion.79 = (f32[1,4,12,96,128]{4,3,0,2,1:T(8,128)S(1)}, f32[1,4,12,96,128]{4,3,0,2,1:T(8,128)S(1)}) fusion(f32[2,4,12,96,128]{4,3,0,2,1:T(8,128)} %fusion.29), kind=kLoop, calls=%fused_computation.95 | loop fusion | bytes 9437184 | tf_op jit(solution)/shard_map/slice | solution.py:69
  (34 shorter events, 11.6 us)
Async XLA Ops:
  0.0 31.0 %collective-permute-start = (bf16[2,2,12,96,128]{4,3,2,1,0:T(8,128)(2,1)}, bf16[2,2,12,96,128]{4,3,2,1,0:T(8,128)(2,1)S(1)}, u32[]{:S(2)}, u32[]{:S(2)}) collective-permute-start(bf16[2,2,12,96,128]{4,3,2,1,0:T(8,128)(2,1)} %bitcast.174), channel_id=1, source_target_pairs={{0,128},{128,256},{256,384},{384,0},{1,129},{129,257},{257,385},{3... | collective-permute-start | bytes 3538952 | tf_op jit(solution)/shard_map/ppermute | solution.py:11
  31.0 32.2 %collective-permute-start.1 = (bf16[2,2,12,96,128]{4,3,2,1,0:T(8,128)(2,1)S(1)}, bf16[2,2,12,96,128]{4,3,2,1,0:T(8,128)(2,1)S(1)}, u32[]{:S(2)}, u32[]{:S(2)}) collective-permute-start(bf16[2,2,12,96,128]{4,3,2,1,0:T(8,128)(2,1)S(1)} %collective-permute-done), channel_id=1, source_target_pairs={{0,32},{32,64},{64,96},{96,0},{1,33},{33,65},{65,97},{97,1},{2,34}... | collective-permute-start | bytes 3538952 | tf_op jit(solution)/shard_map/ppermute | solution.py:11
  63.3 33.5 %collective-permute-start.2 = (bf16[2,2,12,96,128]{4,3,2,1,0:T(8,128)(2,1)S(1)}, bf16[2,2,12,96,128]{4,3,2,1,0:T(8,128)(2,1)S(1)}, u32[]{:S(2)}, u32[]{:S(2)}) collective-permute-start(bf16[2,2,12,96,128]{4,3,2,1,0:T(8,128)(2,1)S(1)} %collective-permute-done.1), channel_id=1, source_target_pairs={{0,8},{8,16},{16,24},{24,0},{1,9},{9,17},{17,25},{25,1},{2,10},{10... | collective-permute-start | bytes 3538952 | tf_op jit(solution)/shard_map/ppermute | solution.py:11
  96.8 1.1 copy-start.1
  105.9 6.8 %copy-start.2 = (bf16[96,12,128]{2,0,1:T(8,128)(2,1)S(1)}, bf16[96,12,128]{2,0,1:T(8,128)(2,1)}, u32[]{:S(2)}) copy-start(bf16[96,12,128]{2,0,1:T(8,128)(2,1)} %param.7) | copy-start | bytes 884740
  105.9 61.6 %all-to-all-start = ((bf16[2,4,12,96,128]{4,0,2,1,3:T(2,128)(2,1)}), bf16[2,4,12,96,128]{4,0,2,1,3:T(2,128)(2,1)S(1)}, u32[]{:S(2)}, u32[]{:S(2)}) async-start(bf16[2,4,12,96,128]{4,0,2,1,3:T(2,128)(2,1)} %copy.9), calls=%async_computation | async-start | bytes 4718592 | tf_op jit(solution)/shard_map/all_to_all | solution.py:54
  168.7 1.1 copy-start.3
  168.7 1.1 copy-start.4
  168.7 1.1 copy-start.5
  168.7 1.1 copy-start.6
  178.1 3.8 %copy-start.7 = (bf16[1,1,1,2]{3,2,1,0:T(2,128)(2,1)S(1)}, bf16[1,1,1,2]{3,2,1,0:T(2,128)(2,1)}, u32[]{:S(2)}) copy-start(bf16[1,1,1,2]{3,2,1,0:T(2,128)(2,1)} %param.6) | copy-start | bytes 16
  178.1 61.0 %all-to-all-start.1 = ((bf16[2,4,96,12,128]{4,0,3,1,2:T(2,128)(2,1)}), bf16[2,4,96,12,128]{4,0,3,1,2:T(2,128)(2,1)S(1)}, u32[]{:S(2)}, u32[]{:S(2)}) async-start(bf16[2,4,96,12,128]{4,0,3,1,2:T(2,128)(2,1)} %copy.13), calls=%async_computation.1 | async-start | bytes 4718592 | tf_op jit(solution)/shard_map/all_to_all | solution.py:60
  181.9 7.1 %collective-permute-start.3 = (bf16[2]{0:T(256)(128)(2,1)S(1)}, bf16[2]{0:T(256)(128)(2,1)S(1)}, u32[]{:S(2)}, u32[]{:S(2)}) collective-permute-start(bf16[2]{0:T(256)(128)(2,1)S(1)} %bitcast.175), channel_id=1, source_target_pairs={{0,128},{128,256},{256,384},{384,0},{1,129},{129,257},{257,385},{3... | collective-permute-start | bytes 20 | tf_op jit(solution)/shard_map/ppermute | solution.py:11
  188.9 5.8 %collective-permute-start.4 = (bf16[2]{0:T(256)(128)(2,1)S(1)}, bf16[2]{0:T(256)(128)(2,1)S(1)}, u32[]{:S(2)}, u32[]{:S(2)}) collective-permute-start(bf16[2]{0:T(256)(128)(2,1)S(1)} %collective-permute-done.3), channel_id=1, source_target_pairs={{0,32},{32,64},{64,96},{96,0},{1,33},{33,65},{65,97},{97,1},{2,34}... | collective-permute-start | bytes 20 | tf_op jit(solution)/shard_map/ppermute | solution.py:11
  194.7 4.6 %collective-permute-start.5 = (bf16[2]{0:T(256)(128)(2,1)S(1)}, bf16[2]{0:T(256)(128)(2,1)S(1)}, u32[]{:S(2)}, u32[]{:S(2)}) collective-permute-start(bf16[2]{0:T(256)(128)(2,1)S(1)} %collective-permute-done.4), channel_id=1, source_target_pairs={{0,8},{8,16},{16,24},{24,0},{1,9},{9,17},{17,25},{25,1},{2,10},{10... | collective-permute-start | bytes 20 | tf_op jit(solution)/shard_map/ppermute | solution.py:11
  245.8 2.8 %copy-start = (f32[2,12,96,128]{3,2,1,0:T(8,128)S(1)}, f32[2,12,96,128]{3,2,1,0:T(8,128)}, u32[]{:S(2)}) copy-start(f32[2,12,96,128]{3,2,1,0:T(8,128)} %get-tuple-element.12) | copy-start | bytes 3538948
where the time goes:
time: 253 us; the launch traced here: 251 us
  waiting for transfers between devices  170 us (67%)
  starting transfers between devices  42.1 us (17%)
  local copies, waits for them, and re-layouts  16.4 us (6%)
  other arithmetic  11.3 us (4%)
  matrix products  10.7 us (4%)
    ppermute x6, waiting for transfers between devices, shifted(): lax.ppermute(value, axis, [(i, (i + by) % size) for i in range(size)])  78.1 us
    all_to_all x1, waiting for transfers between devices, shards(): lax.all_to_all(second, 'fft', split_axis=3, concat_axis=2, tiled=True)  54.7 us
    all_to_all x1, waiting for transfers between devices, shards(): lax.all_to_all(back_one, 'fft', split_axis=2, concat_axis=3, tiled=True)  37.2 us
    ppermute x6, starting transfers between devices, shifted(): lax.ppermute(value, axis, [(i, (i + by) % size) for i in range(size)])  31.6 us
    dot_general x3, matrix products, transform(): return jnp.einsum(form, table, field, preferred_element_type=jnp.float32)  10.7 us
    all_to_all x1, starting transfers between devices, shards(): lax.all_to_all(second, 'fft', split_axis=3, concat_axis=2, tiled=True)  6.77 us
  transfers between devices with their start and end apart: 8, of which 8 were waited for; matrix products, arithmetic and copies ran while one was open for 3% of the time, Pallas kernels for 0%

commit v1 on v0

v1 whole, which is shorter than its diff:
```python
import functools
import math

import jax
import jax.numpy as jnp
import ml_dtypes
import numpy as np
from jax import lax
from jax.experimental import pallas as pl
from jax.experimental.pallas import tpu as pltpu
from jax.sharding import PartitionSpec as P

MESH = pl.DeviceIdType.MESH
CHUNK = 4
GROUP = 4
TILE = CHUNK * GROUP


def dft_table(length, sign):
    index = np.arange(length)
    theta = (index[:, None] * index[None, :] % length) * (2.0 * math.pi / length)
    factor = 1.0 / math.sqrt(length)
    cosine = np.cos(theta) * factor
    sine = np.sin(theta) * (sign * factor)
    return np.stack([np.stack([cosine, -sine]), np.stack([sine, cosine])])


def tables(ring, planes, width_b, width_c):
    width_a = ring * planes
    slab = width_b // ring
    chunks = planes // CHUNK

    def c_table(sign):
        table = dft_table(width_c, sign)
        return table.transpose(1, 3, 0, 2).reshape(2 * width_c, 2 * width_c)

    forward = dft_table(width_b, -1.0).reshape(2, 2, ring, slab, width_b)
    b_forward = forward.transpose(2, 0, 3, 1, 4).reshape(2 * width_b, 2 * width_b)
    inverse = dft_table(width_b, 1.0).reshape(2, 2, width_b, ring, slab)
    b_inverse = inverse.transpose(0, 2, 3, 1, 4).reshape(2 * width_b, 2 * width_b)

    same = np.eye(GROUP)
    forward = dft_table(width_a, -1.0).reshape(2, 2, width_a, ring, chunks, CHUNK)
    a_forward = np.einsum("oikyja,gh->ogkjyiha", forward, same)
    a_forward = a_forward.reshape(2 * GROUP * width_a, 2 * GROUP * width_a)
    inverse = dft_table(width_a, 1.0).reshape(2, 2, ring, chunks, CHUNK, width_a)
    a_inverse = np.einsum("oiyjak,gh->jyogaihk", inverse, same)
    a_inverse = a_inverse.reshape(2 * GROUP * width_a, 2 * GROUP * width_a)
    return [
        t.astype(ml_dtypes.bfloat16)
        for t in (c_table(-1.0), c_table(1.0), b_forward, b_inverse, a_forward, a_inverse)
    ]


def dot(x, y):
    return jnp.dot(x, y, preferred_element_type=jnp.float32)


def kernel_body(
    dims,
    occ_hbm, tgt_hbm, w_ref, ker_hbm, c1_hbm, c2_hbm, b1_hbm, b2_hbm, a1_hbm, a2_hbm,
    out_hbm,
    occ, tgt, ker, c1, c2, b1, b2, a1, a2, w_own, w_got,
    ker_rows, ker_t, mixed, send1, recv1, send2, recv2, acc, out,
    load_sem, shift_send, shift_recv, w_send, w_recv,
    send1_sem, recv1_sem, send2_sem, recv2_sem, out_sem,
):
    sizes, bands, targets, planes, width_b, width_c = dims
    ring = sizes["fft"]
    chunks = planes // CHUNK
    slab = width_b // ring
    groups = slab // GROUP
    width_a = ring * planes
    rows = CHUNK * width_b
    me = lax.axis_index("fft")

    def moved(by):
        return {
            axis: lax.rem(lax.axis_index(axis) + (sizes[axis] + by), sizes[axis])
            for axis in ("kx", "ky", "kz")
        }

    ahead, behind = moved(1), moved(-1)
    order = [d for pair in zip(range(ring // 2, 0, -1), range(ring // 2, ring)) for d in pair]
    order = list(dict.fromkeys(order))

    def partner(d):
        return lax.rem(me + d, ring)

    barrier = pltpu.get_barrier_semaphore()
    for device in (ahead, behind):
        pl.semaphore_signal(barrier, inc=1, device_id=device, device_id_type=MESH)
    for d in order:
        pl.semaphore_signal(barrier, inc=1, device_id={"fft": partner(d)}, device_id_type=MESH)

    loads = [
        pltpu.make_async_copy(src, dst, load_sem.at[i])
        for i, (src, dst) in enumerate(
            (
                (tgt_hbm, tgt), (c1_hbm, c1), (b1_hbm, b1), (ker_hbm, ker),
                (a1_hbm, a1), (a2_hbm, a2), (b2_hbm, b2), (c2_hbm, c2),
            )
        )
    ]
    for load in loads:
        load.start()
    for m in range(bands):
        w_own[m] = jnp.broadcast_to(
            w_ref[:, m : m + 1].astype(jnp.float32), w_own.shape[1:]
        ).astype(jnp.bfloat16)

    pl.semaphore_wait(barrier, 2 + ring - 1)

    def shift(m, j):
        part = (slice(None), m, pl.ds(j * CHUNK, CHUNK))
        return pltpu.make_async_remote_copy(
            src_ref=occ_hbm.at[part],
            dst_ref=occ.at[part],
            send_sem=shift_send.at[m, j],
            recv_sem=shift_recv.at[m, j],
            device_id=ahead,
            device_id_type=MESH,
        )

    w_copy = pltpu.make_async_remote_copy(
        src_ref=w_own, dst_ref=w_got, send_sem=w_send, recv_sem=w_recv,
        device_id=ahead, device_id_type=MESH,
    )
    for m in range(bands):
        for j in range(chunks):
            shift(m, j).start()
    w_copy.start()

    def scatter(p, j, send, recv, send_sem, recv_sem):
        for d in order:
            to = partner(d)
            pltpu.make_async_remote_copy(
                src_ref=send.at[p, j, to],
                dst_ref=recv.at[p, j, me],
                send_sem=send_sem.at[p, j],
                recv_sem=recv_sem.at[p, j],
                device_id={"fft": to},
                device_id_type=MESH,
            ).start()
        pltpu.make_async_copy(send.at[p, j, me], recv.at[p, j, me], recv_sem.at[p, j]).start()

    def gathered(p, j, recv, recv_sem):
        pltpu.make_async_copy(recv.at[p, j], recv.at[p, j], recv_sem.at[p, j]).wait()

    loads[3].wait()
    for k in range(width_a):
        ker_rows[pl.ds(k * 2 * 8, slab), :] = ker[k].astype(jnp.float32)
    for b in range(slab):
        ker_t[b // GROUP, pl.ds(b % GROUP * width_a, width_a), :] = ker_rows[
            pl.ds(b, width_a, stride=2 * 8), :
        ]

    for i in (0, 1, 2):
        loads[i].wait()

    def forward(step, _):
        m, j = step // chunks, lax.rem(step, chunks)
        shift(m, j).wait_recv()
        here = pl.ds(j * CHUNK, CHUNK)
        o_re = occ[0, m, here].reshape(rows, width_c).astype(jnp.float32)
        o_im = occ[1, m, here].reshape(rows, width_c).astype(jnp.float32)
        for n in range(targets):
            p = m * targets + n
            t_re = tgt[0, n, here].reshape(rows, width_c).astype(jnp.float32)
            t_im = tgt[1, n, here].reshape(rows, width_c).astype(jnp.float32)
            pair = jnp.concatenate(
                [
                    (o_re * t_re + o_im * t_im).astype(jnp.bfloat16),
                    (o_re * t_im - o_im * t_re).astype(jnp.bfloat16),
                ],
                axis=1,
            )
            first = dot(pair, c1[...]).astype(jnp.bfloat16)
            for a in range(0, CHUNK, 2):
                both = [first[k * width_b : (k + 1) * width_b] for k in (a, a + 1)]
                lines = jnp.concatenate(
                    [
                        jnp.concatenate([x[:, :width_c] for x in both], axis=1),
                        jnp.concatenate([x[:, width_c:] for x in both], axis=1),
                    ],
                    axis=0,
                )
                second = dot(b1[...], lines)
                mixed[pl.ds(a, 2 * width_b, stride=CHUNK), :] = second[:, :width_c]
                mixed[pl.ds(a + 1, 2 * width_b, stride=CHUNK), :] = second[:, width_c:]
            send1[p, j] = mixed[...].astype(jnp.bfloat16).reshape(send1.shape[2:])
            scatter(p, j, send1, recv1, send1_sem, recv1_sem)
        return 0

    lax.fori_loop(0, bands * chunks, forward, 0)

    for i in (4, 5, 6, 7):
        loads[i].wait()

    def middle(p, _):
        for j in range(chunks):
            gathered(p, j, recv1, recv1_sem)
        lines = jnp.concatenate(
            [
                recv1[p, :, :, :, g * TILE : (g + 1) * TILE, :].reshape(2 * GROUP * width_a, width_c)
                for g in range(groups)
            ],
            axis=1,
        )
        spectrum = dot(a1[...], lines)
        half = GROUP * width_a
        screened = jnp.concatenate(
            [
                jnp.concatenate(
                    [
                        spectrum[i * half : (i + 1) * half, g * width_c : (g + 1) * width_c] * ker_t[g]
                        for g in range(groups)
                    ],
                    axis=1,
                ).astype(jnp.bfloat16)
                for i in range(2)
            ],
            axis=0,
        )
        back = dot(a2[...], screened).astype(jnp.bfloat16)
        for g in range(groups):
            send2[p, :, :, :, g * TILE : (g + 1) * TILE, :] = back[
                :, g * width_c : (g + 1) * width_c
            ].reshape(chunks, ring, 2, TILE, width_c)
        for j in range(chunks):
            scatter(p, j, send2, recv2, send2_sem, recv2_sem)
        return 0

    lax.fori_loop(0, bands * targets, middle, 0)

    w_copy.wait_recv()

    def backward(m, step):
        n, j = step // chunks, lax.rem(step, chunks)
        p = m * targets + n
        gathered(p, j, recv2, recv2_sem)
        mixed[...] = recv2[p, j].reshape(mixed.shape).astype(jnp.float32)
        two = []
        for a in range(0, CHUNK, 2):
            lines = jnp.concatenate(
                [mixed[pl.ds(k, 2 * width_b, stride=CHUNK), :] for k in (a, a + 1)], axis=1
            ).astype(jnp.bfloat16)
            done = dot(b2[...], lines).astype(jnp.bfloat16)
            for k in range(2):
                cut = done[:, k * width_c : (k + 1) * width_c]
                two.append(jnp.concatenate([cut[:width_b], cut[width_b:]], axis=1))
        potential = dot(jnp.concatenate(two, axis=0), c2[...])
        v_re, v_im = potential[:, :width_c], potential[:, width_c:]
        here = pl.ds(j * CHUNK, CHUNK)
        scale = w_got[m].astype(jnp.float32)[:1]
        o_re = occ[0, m, here].reshape(rows, width_c).astype(jnp.float32) * scale
        o_im = occ[1, m, here].reshape(rows, width_c).astype(jnp.float32) * scale
        sums = (o_re * v_re - o_im * v_im, o_re * v_im + o_im * v_re)
        for i in range(2):
            if m > 0:
                total = acc[i, n, j] + sums[i]
            else:
                total = sums[i]
            if m == bands - 1:
                out[i, n, here] = (-0.25 * total).astype(jnp.bfloat16).reshape(
                    CHUNK, width_b, width_c
                )
            else:
                acc[i, n, j] = total
        if m == bands - 1:
            store(n, j).start()
        return 0

    def store(n, j):
        part = (slice(None), n, pl.ds(j * CHUNK, CHUNK))
        return pltpu.make_async_copy(out.at[part], out_hbm.at[part], out_sem.at[n, j])

    for m in range(bands):
        lax.fori_loop(0, targets * chunks, lambda step, _, m=m: backward(m, step), 0)

    w_copy.wait_send()

    def drain_shift(step, _):
        shift(step // chunks, lax.rem(step, chunks)).wait_send()
        return 0

    lax.fori_loop(0, bands * chunks, drain_shift, 0)

    def drain(step, _):
        p, j = step // chunks, lax.rem(step, chunks)
        for send, sem in ((send1, send1_sem), (send2, send2_sem)):
            gone = send.at[p, j, pl.ds(0, ring - 1)]
            pltpu.make_async_copy(gone, gone, sem.at[p, j]).wait()
        return 0

    lax.fori_loop(0, bands * targets * chunks, drain, 0)

    def drain_out(step, _):
        store(step // chunks, lax.rem(step, chunks)).wait()
        return 0

    lax.fori_loop(0, targets * chunks, drain_out, 0)


def shards(occupied, targets, weights, kernel, sizes):
    occ = occupied[0, 0, 0]
    tgt = targets[0, 0, 0]
    bands, tgts = occ.shape[1], tgt.shape[1]
    planes, width_b, width_c = occ.shape[2:]
    ring = sizes["fft"]
    width_a = ring * planes
    slab = width_b // ring
    chunks = planes // CHUNK
    groups = slab // GROUP
    pairs = bands * tgts
    constants = [jnp.asarray(t) for t in tables(ring, planes, width_b, width_c)]
    bf16, f32 = jnp.bfloat16, jnp.float32
    blocks = (pairs, chunks, ring, 2, slab * CHUNK, width_c)
    any_space = pl.BlockSpec(memory_space=pl.ANY)
    result = pl.pallas_call(
        functools.partial(kernel_body, (sizes, bands, tgts, planes, width_b, width_c)),
        out_shape=jax.ShapeDtypeStruct(tgt.shape, bf16),
        in_specs=[any_space, any_space, pl.BlockSpec(memory_space=pltpu.VMEM)] + [any_space] * 7,
        out_specs=any_space,
        scratch_shapes=[
            pltpu.VMEM(occ.shape, bf16),
            pltpu.VMEM(tgt.shape, bf16),
            pltpu.VMEM(kernel.shape, bf16),
            *[pltpu.VMEM(t.shape, bf16) for t in constants],
            pltpu.VMEM((bands, 16, width_c), bf16),
            pltpu.VMEM((bands, 16, width_c), bf16),
            pltpu.VMEM((width_a * 16, width_c), f32),
            pltpu.VMEM((groups, GROUP * width_a, width_c), f32),
            pltpu.VMEM((2 * width_b * CHUNK, width_c), f32),
            *[pltpu.VMEM(blocks, bf16)] * 4,
            pltpu.VMEM((2, tgts, chunks, CHUNK * width_b, width_c), f32),
            pltpu.VMEM(tgt.shape, bf16),
            pltpu.SemaphoreType.DMA((8,)),
            pltpu.SemaphoreType.DMA((bands, chunks)),
            pltpu.SemaphoreType.DMA((bands, chunks)),
            pltpu.SemaphoreType.DMA,
            pltpu.SemaphoreType.DMA,
            *[pltpu.SemaphoreType.DMA((pairs, chunks))] * 4,
            pltpu.SemaphoreType.DMA((tgts, chunks)),
        ],
        compiler_params=pltpu.CompilerParams(
            collective_id=0, has_side_effects=True, vmem_limit_bytes=56 << 20
        ),
    )(occ, tgt, weights.reshape(1, bands), kernel, *constants)
    return result[None, None, None]


def solution(mesh):
    return jax.shard_map(
        functools.partial(shards, sizes=dict(mesh.shape)),
        mesh=mesh,
        in_specs=(
            P("kx", "ky", "kz", None, None, "fft", None, None),
            P("kx", "ky", "kz", None, None, "fft", None, None),
            P("kx", "ky", "kz", None),
            P(None, "fft", None),
        ),
        out_specs=P("kx", "ky", "kz", None, None, "fft", None, None),
        check_vma=False,
    )
```

time: 253 us -> 132 us (0.52)
  waiting for transfers between devices: 170 us -> 0 us
  Pallas kernels: 0 us -> 128 us
  starting transfers between devices: 42.1 us -> 0 us
  local copies, waits for them, and re-layouts: 16.4 us -> 4.19 us
  other arithmetic: 11.3 us -> 0 us
  matrix products: 10.7 us -> 0 us
    pallas_call x0 -> x1, Pallas kernels: none -> 128 us  [shards(): pl.pallas_call(functools.partial(kernel_body, (sizes, bands, tgts, planes...]
    all_to_all x2 -> x0, waiting for transfers between devices: 92 us -> none  [the longest x1 54.7 us: shards(): lax.all_to_all(second, 'fft', split_axis=3, concat_axis=2, tiled=True)]
    ppermute x6 -> x0, waiting for transfers between devices: 78.1 us -> none  [shifted(): lax.ppermute(value, axis, [(i, (i + by) % size) for i in range(size)])]
    ppermute x6 -> x0, starting transfers between devices: 31.6 us -> none  [shifted(): lax.ppermute(value, axis, [(i, (i + by) % size) for i in range(size)])]
    dot_general x3 -> x0, matrix products: 10.7 us -> none  [transform(): return jnp.einsum(form, table, field, preferred_element_type=jnp.float32)]
    all_to_all x2 -> x0, starting transfers between devices: 10.5 us -> none  [the longest x1 6.77 us: shards(): lax.all_to_all(second, 'fft', split_axis=3, concat_axis=2, tiled=True)]
    convert_element_type x2 -> x0, local copies, waits for them, and re-layouts: 8.18 us -> none  [the longest x1 4.92 us: shards(): transform(screened, inverse_a, 'oikj,ipjbc->opkbc').astype(jnp.bfloat16)]
    another operation x9 -> x0, other arithmetic: 4.6 us -> none
  transfers between devices with their start and end apart: 8 -> 0, of which waited for: 8 -> 0; matrix products, arithmetic and copies ran while one was open for 3% -> 0% of each run, Pallas kernels for 0% -> 0%
where the time goes in v1:
time: 132 us
  Pallas kernels  128 us (97%)
  local copies, waits for them, and re-layouts  4.19 us (3%)
    pallas_call x1, Pallas kernels, shards(): pl.pallas_call(functools.partial(kernel_body, (sizes, bands, tgts, planes...  128 us
    unnamed x2, local copies, waits for them, and re-layouts  4.19 us

profile of v1, /device:TPU:1, one launch (start us, length us, event | category | flops | bytes accessed | tf_op | source)
XLA Modules:
  0.0 132.2 jit_solution(14871361089455610728)
XLA Ops:
  0.0 1.8 %copy.11.ker_hbm = bf16[96,12,128]{2,1,0:T(8,128)(2,1)} copy(bf16[96,12,128]{2,0,1:T(8,128)(2,1)} %param.13) | data formatting | bytes 589824 | tf_op args[3]
  1.8 128.0 %shard_map.100 = bf16[2,2,12,96,128]{4,3,2,1,0:T(8,128)(2,1)} custom-call(bf16[2,2,12,96,128]{4,3,2,1,0:T(8,128)(2,1)} %bitcast.5, bf16[2,2,12,96,128]{4,3,2,1,0:T(8,128)(2,1)} %bitcast.6, bf16[1,2]{1,0:T(2,128)(2,1)} %bitcast.7, bf16[96,12,128]{2,1,0:T(8,128)(2,1)} %copy.11.ker_hbm, bf16[256,256]{1,0:T(8,128)(2,1)} %constant.12.clone.c1_hbm, ...), custom_call_target="tpu_custom_call" | custom-call | tf_op jit(solution)/shard_map/pallas_call | solution.py:320
  129.8 2.4 %copy.13 = bf16[1,1,1,2,2,12,96,128]{7,6,5,4,3,2,1,0:T(8,128)(2,1)} copy(bf16[1,1,1,2,2,12,96,128]{7,6,5,4,3,2,1,0:T(8,128)(2,1)} %bitcast.4) | data formatting | bytes 2359296

commit v2 on v1

--- a/solution.py
+++ b/solution.py
@@ -11,9 +11,9 @@
 from jax.sharding import PartitionSpec as P
 
 MESH = pl.DeviceIdType.MESH
-CHUNK = 4
+CHUNK = 2
 GROUP = 4
-TILE = CHUNK * GROUP
+TILE = GROUP * 2 * CHUNK
 
 
 def dft_table(length, sign):
@@ -35,16 +35,16 @@
         return table.transpose(1, 3, 0, 2).reshape(2 * width_c, 2 * width_c)
 
     forward = dft_table(width_b, -1.0).reshape(2, 2, ring, slab, width_b)
-    b_forward = forward.transpose(2, 0, 3, 1, 4).reshape(2 * width_b, 2 * width_b)
+    b_forward = forward.transpose(2, 3, 0, 1, 4).reshape(2 * width_b, 2 * width_b)
     inverse = dft_table(width_b, 1.0).reshape(2, 2, width_b, ring, slab)
-    b_inverse = inverse.transpose(0, 2, 3, 1, 4).reshape(2 * width_b, 2 * width_b)
+    b_inverse = inverse.transpose(0, 2, 3, 4, 1).reshape(2 * width_b, 2 * width_b)
 
     same = np.eye(GROUP)
     forward = dft_table(width_a, -1.0).reshape(2, 2, width_a, ring, chunks, CHUNK)
-    a_forward = np.einsum("oikyja,gh->ogkjyiha", forward, same)
+    a_forward = np.einsum("oikyja,gh->ogkjyhia", forward, same)
     a_forward = a_forward.reshape(2 * GROUP * width_a, 2 * GROUP * width_a)
     inverse = dft_table(width_a, 1.0).reshape(2, 2, ring, chunks, CHUNK, width_a)
-    a_inverse = np.einsum("oiyjak,gh->jyogaihk", inverse, same)
+    a_inverse = np.einsum("oiyjak,gh->jygoaihk", inverse, same)
     a_inverse = a_inverse.reshape(2 * GROUP * width_a, 2 * GROUP * width_a)
     return [
         t.astype(ml_dtypes.bfloat16)
@@ -61,8 +61,8 @@
     occ_hbm, tgt_hbm, w_ref, ker_hbm, c1_hbm, c2_hbm, b1_hbm, b2_hbm, a1_hbm, a2_hbm,
     out_hbm,
     occ, tgt, ker, c1, c2, b1, b2, a1, a2, w_own, w_got,
-    ker_rows, ker_t, mixed, send1, recv1, send2, recv2, acc, out,
-    load_sem, shift_send, shift_recv, w_send, w_recv,
+    mixed, send1, recv1, send2, recv2, acc, out,
+    ready, load_sem, shift_send, shift_recv, w_send, w_recv,
     send1_sem, recv1_sem, send2_sem, recv2_sem, out_sem,
 ):
     sizes, bands, targets, planes, width_b, width_c = dims
@@ -87,11 +87,20 @@
     def partner(d):
         return lax.rem(me + d, ring)
 
+    place = lax.axis_index("kz")
+    asks = place == sizes["kz"] // 2
+    asked = place == sizes["kz"] // 2 - 1
     barrier = pltpu.get_barrier_semaphore()
-    for device in (ahead, behind):
-        pl.semaphore_signal(barrier, inc=1, device_id=device, device_id_type=MESH)
     for d in order:
         pl.semaphore_signal(barrier, inc=1, device_id={"fft": partner(d)}, device_id_type=MESH)
+
+    @pl.when(jnp.logical_not(asks))
+    def _():
+        pl.semaphore_signal(barrier, inc=1, device_id=behind, device_id_type=MESH)
+
+    @pl.when(asked)
+    def _():
+        pl.semaphore_signal(barrier, inc=1, device_id=ahead, device_id_type=MESH)
 
     loads = [
         pltpu.make_async_copy(src, dst, load_sem.at[i])
@@ -109,7 +118,15 @@
             w_ref[:, m : m + 1].astype(jnp.float32), w_own.shape[1:]
         ).astype(jnp.bfloat16)
 
-    pl.semaphore_wait(barrier, 2 + ring - 1)
+    pl.semaphore_wait(barrier, ring - 1 + jnp.where(asked, 0, 1) + jnp.where(asks, 1, 0))
+
+    @pl.when(asks)
+    def _():
+        pl.semaphore_signal(ready, inc=1, device_id=behind, device_id_type=MESH)
+
+    @pl.when(asked)
+    def _():
+        pl.semaphore_wait(ready, 1)
 
     def shift(m, j):
         part = (slice(None), m, pl.ds(j * CHUNK, CHUNK))
@@ -147,24 +164,16 @@
     def gathered(p, j, recv, recv_sem):
         pltpu.make_async_copy(recv.at[p, j], recv.at[p, j], recv_sem.at[p, j]).wait()
 
-    loads[3].wait()
-    for k in range(width_a):
-        ker_rows[pl.ds(k * 2 * 8, slab), :] = ker[k].astype(jnp.float32)
-    for b in range(slab):
-        ker_t[b // GROUP, pl.ds(b % GROUP * width_a, width_a), :] = ker_rows[
-            pl.ds(b, width_a, stride=2 * 8), :
-        ]
-
     for i in (0, 1, 2):
         loads[i].wait()
 
-    def forward(step, _):
-        m, j = step // chunks, lax.rem(step, chunks)
-        shift(m, j).wait_recv()
+    def forward(m, wanted, j):
+        if 0 in wanted:
+            shift(m, j).wait_recv()
         here = pl.ds(j * CHUNK, CHUNK)
         o_re = occ[0, m, here].reshape(rows, width_c).astype(jnp.float32)
         o_im = occ[1, m, here].reshape(rows, width_c).astype(jnp.float32)
-        for n in range(targets):
+        for n in wanted:
             p = m * targets + n
             t_re = tgt[0, n, here].reshape(rows, width_c).astype(jnp.float32)
             t_im = tgt[1, n, here].reshape(rows, width_c).astype(jnp.float32)
@@ -192,9 +201,12 @@
             scatter(p, j, send1, recv1, send1_sem, recv1_sem)
         return 0
 
-    lax.fori_loop(0, bands * chunks, forward, 0)
-
-    for i in (4, 5, 6, 7):
+    everything = tuple(range(targets))
+    for m in range(bands):
+        for wanted in (everything,) if m == 0 else tuple((n,) for n in everything):
+            lax.fori_loop(0, chunks, lambda j, _, m=m, wanted=wanted: forward(m, wanted, j), 0)
+
+    for i in (3, 4, 5, 6, 7):
         loads[i].wait()
 
     def middle(p, _):
@@ -202,18 +214,22 @@
             gathered(p, j, recv1, recv1_sem)
         lines = jnp.concatenate(
             [
-                recv1[p, :, :, :, g * TILE : (g + 1) * TILE, :].reshape(2 * GROUP * width_a, width_c)
+                recv1[p, :, :, g * TILE : (g + 1) * TILE, :].reshape(2 * GROUP * width_a, width_c)
                 for g in range(groups)
             ],
             axis=1,
         )
         spectrum = dot(a1[...], lines)
         half = GROUP * width_a
+        factor = [
+            ker[g * GROUP : (g + 1) * GROUP].reshape(half, width_c).astype(jnp.float32)
+            for g in range(groups)
+        ]
         screened = jnp.concatenate(
             [
                 jnp.concatenate(
                     [
-                        spectrum[i * half : (i + 1) * half, g * width_c : (g + 1) * width_c] * ker_t[g]
+                        spectrum[i * half : (i + 1) * half, g * width_c : (g + 1) * width_c] * factor[g]
                         for g in range(groups)
                     ],
                     axis=1,
@@ -224,9 +240,9 @@
         )
         back = dot(a2[...], screened).astype(jnp.bfloat16)
         for g in range(groups):
-            send2[p, :, :, :, g * TILE : (g + 1) * TILE, :] = back[
+            send2[p, :, :, g * TILE : (g + 1) * TILE, :] = back[
                 :, g * width_c : (g + 1) * width_c
-            ].reshape(chunks, ring, 2, TILE, width_c)
+            ].reshape(chunks, ring, TILE, width_c)
         for j in range(chunks):
             scatter(p, j, send2, recv2, send2_sem, recv2_sem)
         return 0
@@ -315,7 +331,7 @@
     pairs = bands * tgts
     constants = [jnp.asarray(t) for t in tables(ring, planes, width_b, width_c)]
     bf16, f32 = jnp.bfloat16, jnp.float32
-    blocks = (pairs, chunks, ring, 2, slab * CHUNK, width_c)
+    blocks = (pairs, chunks, ring, slab * 2 * CHUNK, width_c)
     any_space = pl.BlockSpec(memory_space=pl.ANY)
     result = pl.pallas_call(
         functools.partial(kernel_body, (sizes, bands, tgts, planes, width_b, width_c)),
@@ -325,16 +341,15 @@
         scratch_shapes=[
             pltpu.VMEM(occ.shape, bf16),
             pltpu.VMEM(tgt.shape, bf16),
-            pltpu.VMEM(kernel.shape, bf16),
+            pltpu.VMEM((slab, width_a, width_c), bf16),
             *[pltpu.VMEM(t.shape, bf16) for t in constants],
             pltpu.VMEM((bands, 16, width_c), bf16),
             pltpu.VMEM((bands, 16, width_c), bf16),
-            pltpu.VMEM((width_a * 16, width_c), f32),
-            pltpu.VMEM((groups, GROUP * width_a, width_c), f32),
             pltpu.VMEM((2 * width_b * CHUNK, width_c), f32),
             *[pltpu.VMEM(blocks, bf16)] * 4,
             pltpu.VMEM((2, tgts, chunks, CHUNK * width_b, width_c), f32),
             pltpu.VMEM(tgt.shape, bf16),
+            pltpu.SemaphoreType.REGULAR,
             pltpu.SemaphoreType.DMA((8,)),
             pltpu.SemaphoreType.DMA((bands, chunks)),
             pltpu.SemaphoreType.DMA((bands, chunks)),
@@ -346,7 +361,7 @@
         compiler_params=pltpu.CompilerParams(
             collective_id=0, has_side_effects=True, vmem_limit_bytes=56 << 20
         ),
-    )(occ, tgt, weights.reshape(1, bands), kernel, *constants)
+    )(occ, tgt, weights.reshape(1, bands), kernel.transpose(1, 0, 2), *constants)
     return result[None, None, None]
 
 

time: 132 us -> 127 us (0.962)
  Pallas kernels: 128 us -> 124 us
  local copies, waits for them, and re-layouts: 4.19 us -> 2.36 us
    pallas_call x1, Pallas kernels: 128 us -> 124 us  [shards(): pl.pallas_call(functools.partial(kernel_body, (sizes, bands, tgts, planes...]
    unnamed x2 -> x1, local copies, waits for them, and re-layouts: 4.19 us -> 2.36 us
where the time goes in v2:
time: 127 us; the launch traced here: 126 us
  Pallas kernels  124 us (98%)
  local copies, waits for them, and re-layouts  2.36 us (2%)
    pallas_call x1, Pallas kernels, shards(): pl.pallas_call(functools.partial(kernel_body, (sizes, bands, tgts, planes...  124 us

profile of v2, /device:TPU:1, one launch (start us, length us, event | category | flops | bytes accessed | tf_op | source)
XLA Modules:
  0.0 126.0 jit_solution(1192432435391001159)
XLA Ops:
  0.0 123.6 %shard_map.100 = bf16[2,2,12,96,128]{4,3,2,1,0:T(8,128)(2,1)} custom-call(bf16[2,2,12,96,128]{4,3,2,1,0:T(8,128)(2,1)} %bitcast.6, bf16[2,2,12,96,128]{4,3,2,1,0:T(8,128)(2,1)} %bitcast.7, bf16[1,2]{1,0:T(2,128)(2,1)} %bitcast.9, bf16[12,96,128]{2,1,0:T(8,128)(2,1)} %bitcast.8, bf16[256,256]{1,0:T(8,128)(2,1)} %constant.12.clone.c1_hbm, ...), custom_call_target="tpu_custom_call" | custom-call | tf_op jit(solution)/shard_map/pallas_call | solution.py:336
  123.6 2.4 %copy.12 = bf16[1,1,1,2,2,12,96,128]{7,6,5,4,3,2,1,0:T(8,128)(2,1)} copy(bf16[1,1,1,2,2,12,96,128]{7,6,5,4,3,2,1,0:T(8,128)(2,1)} %bitcast.5) | data formatting | bytes 2359296

commit v3 on v2

--- a/solution.py
+++ b/solution.py
@@ -60,7 +60,7 @@
     dims,
     occ_hbm, tgt_hbm, w_ref, ker_hbm, c1_hbm, c2_hbm, b1_hbm, b2_hbm, a1_hbm, a2_hbm,
     out_hbm,
-    occ, tgt, ker, c1, c2, b1, b2, a1, a2, w_own, w_got,
+    occ, own, tgt, ker, c1, c2, b1, b2, a1, a2, w_own, w_got,
     mixed, send1, recv1, send2, recv2, acc, out,
     ready, load_sem, shift_send, shift_recv, w_send, w_recv,
     send1_sem, recv1_sem, send2_sem, recv2_sem, out_sem,
@@ -107,17 +107,18 @@
         for i, (src, dst) in enumerate(
             (
                 (tgt_hbm, tgt), (c1_hbm, c1), (b1_hbm, b1), (ker_hbm, ker),
-                (a1_hbm, a1), (a2_hbm, a2), (b2_hbm, b2), (c2_hbm, c2),
+                (a1_hbm, a1), (a2_hbm, a2), (b2_hbm, b2), (c2_hbm, c2), (occ_hbm, own),
             )
         )
     ]
-    for load in loads:
+    for load in loads[-1:] + loads[:-1]:
         load.start()
     for m in range(bands):
         w_own[m] = jnp.broadcast_to(
             w_ref[:, m : m + 1].astype(jnp.float32), w_own.shape[1:]
         ).astype(jnp.bfloat16)
 
+    loads[-1].wait()
     pl.semaphore_wait(barrier, ring - 1 + jnp.where(asked, 0, 1) + jnp.where(asks, 1, 0))
 
     @pl.when(asks)
@@ -131,9 +132,9 @@
     def shift(m, j):
         part = (slice(None), m, pl.ds(j * CHUNK, CHUNK))
         return pltpu.make_async_remote_copy(
-            src_ref=occ_hbm.at[part],
+            src_ref=own.at[part],
             dst_ref=occ.at[part],
-            send_sem=shift_send.at[m, j],
+            send_sem=shift_send,
             recv_sem=shift_recv.at[m, j],
             device_id=ahead,
             device_id_type=MESH,
@@ -154,26 +155,26 @@
             pltpu.make_async_remote_copy(
                 src_ref=send.at[p, j, to],
                 dst_ref=recv.at[p, j, me],
-                send_sem=send_sem.at[p, j],
-                recv_sem=recv_sem.at[p, j],
+                send_sem=send_sem,
+                recv_sem=recv_sem,
                 device_id={"fft": to},
                 device_id_type=MESH,
             ).start()
-        pltpu.make_async_copy(send.at[p, j, me], recv.at[p, j, me], recv_sem.at[p, j]).start()
-
-    def gathered(p, j, recv, recv_sem):
-        pltpu.make_async_copy(recv.at[p, j], recv.at[p, j], recv_sem.at[p, j]).wait()
+        pltpu.make_async_copy(send.at[p, j, me], recv.at[p, j, me], recv_sem).start()
+
+    def ended(part, sem):
+        pltpu.make_async_copy(part, part, sem).wait()
 
     for i in (0, 1, 2):
         loads[i].wait()
 
-    def forward(m, wanted, j):
-        if 0 in wanted:
-            shift(m, j).wait_recv()
+    def forward(step, _):
+        m, j = step // chunks, lax.rem(step, chunks)
+        shift(m, j).wait_recv()
         here = pl.ds(j * CHUNK, CHUNK)
         o_re = occ[0, m, here].reshape(rows, width_c).astype(jnp.float32)
         o_im = occ[1, m, here].reshape(rows, width_c).astype(jnp.float32)
-        for n in wanted:
+        for n in range(targets):
             p = m * targets + n
             t_re = tgt[0, n, here].reshape(rows, width_c).astype(jnp.float32)
             t_im = tgt[1, n, here].reshape(rows, width_c).astype(jnp.float32)
@@ -198,20 +199,16 @@
                 mixed[pl.ds(a, 2 * width_b, stride=CHUNK), :] = second[:, :width_c]
                 mixed[pl.ds(a + 1, 2 * width_b, stride=CHUNK), :] = second[:, width_c:]
             send1[p, j] = mixed[...].astype(jnp.bfloat16).reshape(send1.shape[2:])
-            scatter(p, j, send1, recv1, send1_sem, recv1_sem)
+            scatter(p, j, send1, recv1, send1_sem, recv1_sem.at[p])
         return 0
 
-    everything = tuple(range(targets))
-    for m in range(bands):
-        for wanted in (everything,) if m == 0 else tuple((n,) for n in everything):
-            lax.fori_loop(0, chunks, lambda j, _, m=m, wanted=wanted: forward(m, wanted, j), 0)
+    lax.fori_loop(0, bands * chunks, forward, 0)
 
     for i in (3, 4, 5, 6, 7):
         loads[i].wait()
 
     def middle(p, _):
-        for j in range(chunks):
-            gathered(p, j, recv1, recv1_sem)
+        ended(recv1.at[p], recv1_sem.at[p])
         lines = jnp.concatenate(
             [
                 recv1[p, :, :, g * TILE : (g + 1) * TILE, :].reshape(2 * GROUP * width_a, width_c)
@@ -244,17 +241,19 @@
                 :, g * width_c : (g + 1) * width_c
             ].reshape(chunks, ring, TILE, width_c)
         for j in range(chunks):
-            scatter(p, j, send2, recv2, send2_sem, recv2_sem)
+            scatter(p, j, send2, recv2, send2_sem, recv2_sem.at[p, j])
         return 0
 
     lax.fori_loop(0, bands * targets, middle, 0)
 
-    w_copy.wait_recv()
+    w_copy.wait()
+    ended(occ, shift_send)
+    ended(send1.at[:, :, pl.ds(0, ring - 1)], send1_sem)
 
     def backward(m, step):
         n, j = step // chunks, lax.rem(step, chunks)
         p = m * targets + n
-        gathered(p, j, recv2, recv2_sem)
+        ended(recv2.at[p, j], recv2_sem.at[p, j])
         mixed[...] = recv2[p, j].reshape(mixed.shape).astype(jnp.float32)
         two = []
         for a in range(0, CHUNK, 2):
@@ -289,33 +288,13 @@
 
     def store(n, j):
         part = (slice(None), n, pl.ds(j * CHUNK, CHUNK))
-        return pltpu.make_async_copy(out.at[part], out_hbm.at[part], out_sem.at[n, j])
+        return pltpu.make_async_copy(out.at[part], out_hbm.at[part], out_sem)
 
     for m in range(bands):
         lax.fori_loop(0, targets * chunks, lambda step, _, m=m: backward(m, step), 0)
 
-    w_copy.wait_send()
-
-    def drain_shift(step, _):
-        shift(step // chunks, lax.rem(step, chunks)).wait_send()
-        return 0
-
-    lax.fori_loop(0, bands * chunks, drain_shift, 0)
-
-    def drain(step, _):
-        p, j = step // chunks, lax.rem(step, chunks)
-        for send, sem in ((send1, send1_sem), (send2, send2_sem)):
-            gone = send.at[p, j, pl.ds(0, ring - 1)]
-            pltpu.make_async_copy(gone, gone, sem.at[p, j]).wait()
-        return 0
-
-    lax.fori_loop(0, bands * targets * chunks, drain, 0)
-
-    def drain_out(step, _):
-        store(step // chunks, lax.rem(step, chunks)).wait()
-        return 0
-
-    lax.fori_loop(0, targets * chunks, drain_out, 0)
+    ended(send2.at[:, :, pl.ds(0, ring - 1)], send2_sem)
+    ended(out, out_sem)
 
 
 def shards(occupied, targets, weights, kernel, sizes):
@@ -340,6 +319,7 @@
         out_specs=any_space,
         scratch_shapes=[
             pltpu.VMEM(occ.shape, bf16),
+            pltpu.VMEM(occ.shape, bf16),
             pltpu.VMEM(tgt.shape, bf16),
             pltpu.VMEM((slab, width_a, width_c), bf16),
             *[pltpu.VMEM(t.shape, bf16) for t in constants],
@@ -350,13 +330,16 @@
             pltpu.VMEM((2, tgts, chunks, CHUNK * width_b, width_c), f32),
             pltpu.VMEM(tgt.shape, bf16),
             pltpu.SemaphoreType.REGULAR,
-            pltpu.SemaphoreType.DMA((8,)),
+            pltpu.SemaphoreType.DMA((9,)),
+            pltpu.SemaphoreType.DMA,
             pltpu.SemaphoreType.DMA((bands, chunks)),
-            pltpu.SemaphoreType.DMA((bands, chunks)),
-            pltpu.SemaphoreType.DMA,
-            pltpu.SemaphoreType.DMA,
-            *[pltpu.SemaphoreType.DMA((pairs, chunks))] * 4,
-            pltpu.SemaphoreType.DMA((tgts, chunks)),
+            pltpu.SemaphoreType.DMA,
+            pltpu.SemaphoreType.DMA,
+            pltpu.SemaphoreType.DMA,
+            pltpu.SemaphoreType.DMA((pairs,)),
+            pltpu.SemaphoreType.DMA,
+            pltpu.SemaphoreType.DMA((pairs, chunks)),
+            pltpu.SemaphoreType.DMA,
         ],
         compiler_params=pltpu.CompilerParams(
             collective_id=0, has_side_effects=True, vmem_limit_bytes=56 << 20

time: 127 us -> 125 us (0.984)
  no operation moved by 1% of the time
where the time goes in v3:
time: 125 us
  Pallas kernels  123 us (98%)
  local copies, waits for them, and re-layouts  2.36 us (2%)
    pallas_call x1, Pallas kernels, shards(): pl.pallas_call(functools.partial(kernel_body, (sizes, bands, tgts, planes...  123 us

profile of v3, /device:TPU:1, one launch (start us, length us, event | category | flops | bytes accessed | tf_op | source)
XLA Modules:
  0.0 124.9 jit_solution(13060017988804014843)
XLA Ops:
  0.0 122.6 %shard_map.100 = bf16[2,2,12,96,128]{4,3,2,1,0:T(8,128)(2,1)} custom-call(bf16[2,2,12,96,128]{4,3,2,1,0:T(8,128)(2,1)} %bitcast.6, bf16[2,2,12,96,128]{4,3,2,1,0:T(8,128)(2,1)} %bitcast.7, bf16[1,2]{1,0:T(2,128)(2,1)} %bitcast.9, bf16[12,96,128]{2,1,0:T(8,128)(2,1)} %bitcast.8, bf16[256,256]{1,0:T(8,128)(2,1)} %constant.12.clone.c1_hbm, ...), custom_call_target="tpu_custom_call" | custom-call | tf_op jit(solution)/shard_map/pallas_call | solution.py:315
  122.6 2.4 %copy.12 = bf16[1,1,1,2,2,12,96,128]{7,6,5,4,3,2,1,0:T(8,128)(2,1)} copy(bf16[1,1,1,2,2,12,96,128]{7,6,5,4,3,2,1,0:T(8,128)(2,1)} %bitcast.5) | data formatting | bytes 2359296

commit v4 on v3

--- a/solution.py
+++ b/solution.py
@@ -11,9 +11,9 @@
 from jax.sharding import PartitionSpec as P
 
 MESH = pl.DeviceIdType.MESH
-CHUNK = 2
+PAIRED = 2
 GROUP = 4
-TILE = GROUP * 2 * CHUNK
+TILE = GROUP * 2 * PAIRED
 
 
 def dft_table(length, sign):
@@ -28,7 +28,7 @@
 def tables(ring, planes, width_b, width_c):
     width_a = ring * planes
     slab = width_b // ring
-    chunks = planes // CHUNK
+    chunks = planes
 
     def c_table(sign):
         table = dft_table(width_c, sign)
@@ -39,13 +39,12 @@
     inverse = dft_table(width_b, 1.0).reshape(2, 2, width_b, ring, slab)
     b_inverse = inverse.transpose(0, 2, 3, 4, 1).reshape(2 * width_b, 2 * width_b)
 
-    same = np.eye(GROUP)
-    forward = dft_table(width_a, -1.0).reshape(2, 2, width_a, ring, chunks, CHUNK)
-    a_forward = np.einsum("oikyja,gh->ogkjyhia", forward, same)
-    a_forward = a_forward.reshape(2 * GROUP * width_a, 2 * GROUP * width_a)
-    inverse = dft_table(width_a, 1.0).reshape(2, 2, ring, chunks, CHUNK, width_a)
-    a_inverse = np.einsum("oiyjak,gh->jygoaihk", inverse, same)
-    a_inverse = a_inverse.reshape(2 * GROUP * width_a, 2 * GROUP * width_a)
+    same, band = np.eye(GROUP), np.eye(PAIRED)
+    size = 2 * PAIRED * GROUP * width_a
+    forward = dft_table(width_a, -1.0).reshape(2, 2, width_a, ring, chunks)
+    a_forward = np.einsum("oikyj,gh,nq->nogkjyhiq", forward, same, band).reshape(size, size)
+    inverse = dft_table(width_a, 1.0).reshape(2, 2, ring, chunks, width_a)
+    a_inverse = np.einsum("oiyjk,gh,nq->jygonqihk", inverse, same, band).reshape(size, size)
     return [
         t.astype(ml_dtypes.bfloat16)
         for t in (c_table(-1.0), c_table(1.0), b_forward, b_inverse, a_forward, a_inverse)
@@ -67,11 +66,10 @@
 ):
     sizes, bands, targets, planes, width_b, width_c = dims
     ring = sizes["fft"]
-    chunks = planes // CHUNK
+    chunks = planes
     slab = width_b // ring
     groups = slab // GROUP
     width_a = ring * planes
-    rows = CHUNK * width_b
     me = lax.axis_index("fft")
 
     def moved(by):
@@ -130,7 +128,7 @@
         pl.semaphore_wait(ready, 1)
 
     def shift(m, j):
-        part = (slice(None), m, pl.ds(j * CHUNK, CHUNK))
+        part = (slice(None), m, j)
         return pltpu.make_async_remote_copy(
             src_ref=own.at[part],
             dst_ref=occ.at[part],
@@ -171,35 +169,33 @@
     def forward(step, _):
         m, j = step // chunks, lax.rem(step, chunks)
         shift(m, j).wait_recv()
-        here = pl.ds(j * CHUNK, CHUNK)
-        o_re = occ[0, m, here].reshape(rows, width_c).astype(jnp.float32)
-        o_im = occ[1, m, here].reshape(rows, width_c).astype(jnp.float32)
+        o_re, o_im = (occ[i, m, j].astype(jnp.float32) for i in range(2))
+        pairs = []
         for n in range(targets):
-            p = m * targets + n
-            t_re = tgt[0, n, here].reshape(rows, width_c).astype(jnp.float32)
-            t_im = tgt[1, n, here].reshape(rows, width_c).astype(jnp.float32)
-            pair = jnp.concatenate(
-                [
-                    (o_re * t_re + o_im * t_im).astype(jnp.bfloat16),
-                    (o_re * t_im - o_im * t_re).astype(jnp.bfloat16),
-                ],
-                axis=1,
+            t_re, t_im = (tgt[i, n, j].astype(jnp.float32) for i in range(2))
+            pairs.append(
+                jnp.concatenate(
+                    [
+                        (o_re * t_re + o_im * t_im).astype(jnp.bfloat16),
+                        (o_re * t_im - o_im * t_re).astype(jnp.bfloat16),
+                    ],
+                    axis=1,
+                )
             )
-            first = dot(pair, c1[...]).astype(jnp.bfloat16)
-            for a in range(0, CHUNK, 2):
-                both = [first[k * width_b : (k + 1) * width_b] for k in (a, a + 1)]
-                lines = jnp.concatenate(
-                    [
-                        jnp.concatenate([x[:, :width_c] for x in both], axis=1),
-                        jnp.concatenate([x[:, width_c:] for x in both], axis=1),
-                    ],
-                    axis=0,
-                )
-                second = dot(b1[...], lines)
-                mixed[pl.ds(a, 2 * width_b, stride=CHUNK), :] = second[:, :width_c]
-                mixed[pl.ds(a + 1, 2 * width_b, stride=CHUNK), :] = second[:, width_c:]
-            send1[p, j] = mixed[...].astype(jnp.bfloat16).reshape(send1.shape[2:])
-            scatter(p, j, send1, recv1, send1_sem, recv1_sem.at[p])
+        first = dot(jnp.concatenate(pairs, axis=0), c1[...]).astype(jnp.bfloat16)
+        both = [first[n * width_b : (n + 1) * width_b] for n in range(targets)]
+        lines = jnp.concatenate(
+            [
+                jnp.concatenate([x[:, :width_c] for x in both], axis=1),
+                jnp.concatenate([x[:, width_c:] for x in both], axis=1),
+            ],
+            axis=0,
+        )
+        second = dot(b1[...], lines)
+        for n in range(targets):
+            mixed[pl.ds(n, 2 * width_b, stride=targets), :] = second[:, n * width_c : (n + 1) * width_c]
+        send1[m, j] = mixed[...].astype(jnp.bfloat16).reshape(send1.shape[2:])
+        scatter(m, j, send1, recv1, send1_sem, recv1_sem.at[m])
         return 0
 
     lax.fori_loop(0, bands * chunks, forward, 0)
@@ -211,7 +207,7 @@
         ended(recv1.at[p], recv1_sem.at[p])
         lines = jnp.concatenate(
             [
-                recv1[p, :, :, g * TILE : (g + 1) * TILE, :].reshape(2 * GROUP * width_a, width_c)
+                recv1[p, :, :, g * TILE : (g + 1) * TILE, :].reshape(2 * PAIRED * GROUP * width_a, width_c)
                 for g in range(groups)
             ],
             axis=1,
@@ -231,7 +227,7 @@
                     ],
                     axis=1,
                 ).astype(jnp.bfloat16)
-                for i in range(2)
+                for i in range(2 * PAIRED)
             ],
             axis=0,
         )
@@ -244,54 +240,44 @@
             scatter(p, j, send2, recv2, send2_sem, recv2_sem.at[p, j])
         return 0
 
-    lax.fori_loop(0, bands * targets, middle, 0)
+    lax.fori_loop(0, bands, middle, 0)
 
     w_copy.wait()
     ended(occ, shift_send)
     ended(send1.at[:, :, pl.ds(0, ring - 1)], send1_sem)
 
-    def backward(m, step):
-        n, j = step // chunks, lax.rem(step, chunks)
-        p = m * targets + n
-        ended(recv2.at[p, j], recv2_sem.at[p, j])
-        mixed[...] = recv2[p, j].reshape(mixed.shape).astype(jnp.float32)
-        two = []
-        for a in range(0, CHUNK, 2):
-            lines = jnp.concatenate(
-                [mixed[pl.ds(k, 2 * width_b, stride=CHUNK), :] for k in (a, a + 1)], axis=1
-            ).astype(jnp.bfloat16)
-            done = dot(b2[...], lines).astype(jnp.bfloat16)
-            for k in range(2):
-                cut = done[:, k * width_c : (k + 1) * width_c]
-                two.append(jnp.concatenate([cut[:width_b], cut[width_b:]], axis=1))
-        potential = dot(jnp.concatenate(two, axis=0), c2[...])
-        v_re, v_im = potential[:, :width_c], potential[:, width_c:]
-        here = pl.ds(j * CHUNK, CHUNK)
+    def backward(m, j):
+        ended(recv2.at[m, j], recv2_sem.at[m, j])
+        mixed[...] = recv2[m, j].reshape(mixed.shape).astype(jnp.float32)
+        lines = jnp.concatenate(
+            [mixed[pl.ds(n, 2 * width_b, stride=targets), :] for n in range(targets)], axis=1
+        ).astype(jnp.bfloat16)
+        done = dot(b2[...], lines).astype(jnp.bfloat16)
+        cuts = [done[:, n * width_c : (n + 1) * width_c] for n in range(targets)]
+        lines = [jnp.concatenate([cut[:width_b], cut[width_b:]], axis=1) for cut in cuts]
+        potential = dot(jnp.concatenate(lines, axis=0), c2[...])
         scale = w_got[m].astype(jnp.float32)[:1]
-        o_re = occ[0, m, here].reshape(rows, width_c).astype(jnp.float32) * scale
-        o_im = occ[1, m, here].reshape(rows, width_c).astype(jnp.float32) * scale
-        sums = (o_re * v_re - o_im * v_im, o_re * v_im + o_im * v_re)
-        for i in range(2):
-            if m > 0:
-                total = acc[i, n, j] + sums[i]
-            else:
-                total = sums[i]
-            if m == bands - 1:
-                out[i, n, here] = (-0.25 * total).astype(jnp.bfloat16).reshape(
-                    CHUNK, width_b, width_c
-                )
-            else:
-                acc[i, n, j] = total
+        o_re, o_im = (occ[i, m, j].astype(jnp.float32) * scale for i in range(2))
+        for n in range(targets):
+            part = potential[n * width_b : (n + 1) * width_b]
+            v_re, v_im = part[:, :width_c], part[:, width_c:]
+            sums = (o_re * v_re - o_im * v_im, o_re * v_im + o_im * v_re)
+            for i in range(2):
+                total = acc[i, n, j] + sums[i] if m > 0 else sums[i]
+                if m == bands - 1:
+                    out[i, n, j] = (-0.25 * total).astype(jnp.bfloat16)
+                else:
+                    acc[i, n, j] = total
         if m == bands - 1:
-            store(n, j).start()
+            store(j).start()
         return 0
 
-    def store(n, j):
-        part = (slice(None), n, pl.ds(j * CHUNK, CHUNK))
+    def store(j):
+        part = (slice(None), slice(None), j)
         return pltpu.make_async_copy(out.at[part], out_hbm.at[part], out_sem)
 
     for m in range(bands):
-        lax.fori_loop(0, targets * chunks, lambda step, _, m=m: backward(m, step), 0)
+        lax.fori_loop(0, chunks, lambda j, _, m=m: backward(m, j), 0)
 
     ended(send2.at[:, :, pl.ds(0, ring - 1)], send2_sem)
     ended(out, out_sem)
@@ -305,12 +291,11 @@
     ring = sizes["fft"]
     width_a = ring * planes
     slab = width_b // ring
-    chunks = planes // CHUNK
+    chunks = planes
     groups = slab // GROUP
-    pairs = bands * tgts
     constants = [jnp.asarray(t) for t in tables(ring, planes, width_b, width_c)]
     bf16, f32 = jnp.bfloat16, jnp.float32
-    blocks = (pairs, chunks, ring, slab * 2 * CHUNK, width_c)
+    blocks = (bands, chunks, ring, slab * 2 * PAIRED, width_c)
     any_space = pl.BlockSpec(memory_space=pl.ANY)
     result = pl.pallas_call(
         functools.partial(kernel_body, (sizes, bands, tgts, planes, width_b, width_c)),
@@ -325,9 +310,9 @@
             *[pltpu.VMEM(t.shape, bf16) for t in constants],
             pltpu.VMEM((bands, 16, width_c), bf16),
             pltpu.VMEM((bands, 16, width_c), bf16),
-            pltpu.VMEM((2 * width_b * CHUNK, width_c), f32),
+            pltpu.VMEM((2 * width_b * PAIRED, width_c), f32),
             *[pltpu.VMEM(blocks, bf16)] * 4,
-            pltpu.VMEM((2, tgts, chunks, CHUNK * width_b, width_c), f32),
+            pltpu.VMEM((2, tgts, chunks, width_b, width_c), f32),
             pltpu.VMEM(tgt.shape, bf16),
             pltpu.SemaphoreType.REGULAR,
             pltpu.SemaphoreType.DMA((9,)),
@@ -336,9 +321,9 @@
             pltpu.SemaphoreType.DMA,
             pltpu.SemaphoreType.DMA,
             pltpu.SemaphoreType.DMA,
-            pltpu.SemaphoreType.DMA((pairs,)),
-            pltpu.SemaphoreType.DMA,
-            pltpu.SemaphoreType.DMA((pairs, chunks)),
+            pltpu.SemaphoreType.DMA((bands,)),
+            pltpu.SemaphoreType.DMA,
+            pltpu.SemaphoreType.DMA((bands, chunks)),
             pltpu.SemaphoreType.DMA,
         ],
         compiler_params=pltpu.CompilerParams(

time: 125 us -> 125 us (level); the launches traced: 125 us -> 123 us
  Pallas kernels: 123 us -> 121 us
    pallas_call x1, Pallas kernels: 123 us -> 121 us  [shards(): pl.pallas_call(functools.partial(kernel_body, (sizes, bands, tgts, planes...]
where the time goes in v4:
time: 125 us; the launch traced here: 123 us
  Pallas kernels  121 us (97%)
  local copies, waits for them, and re-layouts  2.36 us (2%)
    pallas_call x1, Pallas kernels, shards(): pl.pallas_call(functools.partial(kernel_body, (sizes, bands, tgts, planes...  121 us

profile of v4, /device:TPU:1, one launch (start us, length us, event | category | flops | bytes accessed | tf_op | source)
XLA Modules:
  0.0 122.9 jit_solution(10967825832199714088)
XLA Ops:
  0.0 120.6 %shard_map.100 = bf16[2,2,12,96,128]{4,3,2,1,0:T(8,128)(2,1)} custom-call(bf16[2,2,12,96,128]{4,3,2,1,0:T(8,128)(2,1)} %bitcast.6, bf16[2,2,12,96,128]{4,3,2,1,0:T(8,128)(2,1)} %bitcast.7, bf16[1,2]{1,0:T(2,128)(2,1)} %bitcast.9, bf16[12,96,128]{2,1,0:T(8,128)(2,1)} %bitcast.8, bf16[256,256]{1,0:T(8,128)(2,1)} %constant.12.clone.c1_hbm, ...), custom_call_target="tpu_custom_call" | custom-call | tf_op jit(solution)/shard_map/pallas_call | solution.py:300
  120.6 2.4 %copy.12 = bf16[1,1,1,2,2,12,96,128]{7,6,5,4,3,2,1,0:T(8,128)(2,1)} copy(bf16[1,1,1,2,2,12,96,128]{7,6,5,4,3,2,1,0:T(8,128)(2,1)} %bitcast.5) | data formatting | bytes 2359296

commit v5 on v4

--- a/solution.py
+++ b/solution.py
@@ -123,10 +123,6 @@
     def _():
         pl.semaphore_signal(ready, inc=1, device_id=behind, device_id_type=MESH)
 
-    @pl.when(asked)
-    def _():
-        pl.semaphore_wait(ready, 1)
-
     def shift(m, j):
         part = (slice(None), m, j)
         return pltpu.make_async_remote_copy(
@@ -142,10 +138,18 @@
         src_ref=w_own, dst_ref=w_got, send_sem=w_send, recv_sem=w_recv,
         device_id=ahead, device_id_type=MESH,
     )
-    for m in range(bands):
-        for j in range(chunks):
-            shift(m, j).start()
-    w_copy.start()
+    def send_ahead():
+        def one(step, _):
+            shift(step // chunks, lax.rem(step, chunks)).start()
+            return 0
+
+        lax.fori_loop(0, bands * chunks, one, 0)
+        w_copy.start()
+
+    @pl.when(jnp.logical_not(asked))
+    def _():
+        send_ahead()
+
 
     def scatter(p, j, send, recv, send_sem, recv_sem):
         for d in order:
@@ -168,6 +172,12 @@
 
     def forward(step, _):
         m, j = step // chunks, lax.rem(step, chunks)
+
+        @pl.when(jnp.logical_and(asked, step == 2))
+        def _():
+            pl.semaphore_wait(ready, 1)
+            send_ahead()
+
         shift(m, j).wait_recv()
         o_re, o_im = (occ[i, m, j].astype(jnp.float32) for i in range(2))
         pairs = []

time: 125 us -> 124 us (level)
  no operation moved by 1% of the time
where the time goes in v5:
time: 124 us; the launch traced here: 123 us
  Pallas kernels  121 us (98%)
  local copies, waits for them, and re-layouts  2.36 us (2%)
    pallas_call x1, Pallas kernels, shards(): pl.pallas_call(functools.partial(kernel_body, (sizes, bands, tgts, planes...  121 us

profile of v5, /device:TPU:1, one launch (start us, length us, event | category | flops | bytes accessed | tf_op | source)
XLA Modules:
  0.0 123.0 jit_solution(17734089127017883745)
XLA Ops:
  0.0 120.7 %shard_map.100 = bf16[2,2,12,96,128]{4,3,2,1,0:T(8,128)(2,1)} custom-call(bf16[2,2,12,96,128]{4,3,2,1,0:T(8,128)(2,1)} %bitcast.6, bf16[2,2,12,96,128]{4,3,2,1,0:T(8,128)(2,1)} %bitcast.7, bf16[1,2]{1,0:T(2,128)(2,1)} %bitcast.9, bf16[12,96,128]{2,1,0:T(8,128)(2,1)} %bitcast.8, bf16[256,256]{1,0:T(8,128)(2,1)} %constant.12.clone.c1_hbm, ...), custom_call_target="tpu_custom_call" | custom-call | tf_op jit(solution)/shard_map/pallas_call | solution.py:310
  120.7 2.4 %copy.12 = bf16[1,1,1,2,2,12,96,128]{7,6,5,4,3,2,1,0:T(8,128)(2,1)} copy(bf16[1,1,1,2,2,12,96,128]{7,6,5,4,3,2,1,0:T(8,128)(2,1)} %bitcast.5) | data formatting | bytes 2359296
